TPU v7x, 512 devices: a whole 4x8x8 slice. The times are simulated.
512 devices in a mesh: batch: 32 (over z, x), blk: 16 (over y, core).
Axes of the slice: x: 4, y: 8, z: 8, core: 2. Of those that a mesh axis runs over, the one named last changes fastest.
Arguments:
- points: float32 [1024, 16, 3, 256], P('batch', 'blk'), may hold values from -6 to 6
- centers: float32 [1024, 16, 3, 384], P('batch', 'blk'), may hold values from -6 to 6
- exponents: float32 [1024, 16, 384], P('batch', 'blk'), may hold values from 0.1 to 1
- angular: float32 [1024, 16, 3, 384], P('batch', 'blk'), may hold values from -3 to 3
- grid_weights: float32 [1024, 16, 256], P('batch', 'blk'), may hold values from 0.001 to 0.01
- hartree: float32 [1024, 16, 256], P('batch', 'blk'), may hold values from 0 to 1.7
- load_plan: int32 [16, 1024], P('blk'), may hold values from 0 to 1023, each once within a row
- density_blocks: bfloat16 [256, 128, 128], P('blk'), may hold values from -0.046875 to 0.046875
- pair_lists: int32 [32, 16, 16, 2], P('batch', 'blk'), may hold values from 0 to 15
- batch_pairs: int32 [1024, 16, 9], P('batch', 'blk'), may hold values from 0 to 31, as said below
Outputs:
- hamiltonian: float32 [256, 128, 128], P('blk')
- density: float32 [1024, 16, 256], P('batch', 'blk')
Inputs may be any that keep to these rules, and one draw needn't show every extreme that they name: Each row of load_plan names every storage row of its column once. `pair_lists`: local index of a block pair within the 16 pairs held by one index of blk. `batch_pairs`: entry e of a device's table is the (e % 2)-th block it reads from index e // 2 of blk; every entry of a device's table is named by some pair of its batches.
All inputs are finite; a program needn't handle non-finite values.
Results may differ from a plain program's by a relative error of at most 0.0065.
Values may be sent and summed in bfloat16 or wider, within the bound.
No kernel may reach another device: no remote copies, remote signals or barrier semaphores. Data moves between devices by JAX's collectives and lax.ppermute only.
A program may use at most 64 MiB of HBM per device.

v0:
```python
import jax
import jax.numpy as jnp
from jax import lax
from jax.sharding import PartitionSpec as P

LIST = 3
xc_scale = 0.98474502
soft_square = 0.01


def exchange_potential(grid_rho):
    return -xc_scale * jnp.power(grid_rho * grid_rho + soft_square, 1.0 / 6.0)


def evaluate(points, centers, exponents, angular):
    distance = jnp.zeros(points.shape[:-2] + (points.shape[-1], centers.shape[-1]), jnp.float32)
    angular_part = jnp.ones_like(distance)
    for component in range(3):
        delta = points[..., component, :, None] - centers[..., component, None, :]
        distance = distance + delta * delta
        angular_part = angular_part + angular[..., component, None, :] * delta
    return (jnp.exp(-exponents[..., None, :] * distance) * angular_part).astype(jnp.bfloat16)


def on_device(
    points,
    centers,
    exponents,
    angular,
    grid_weights,
    hartree,
    load_plan,
    density_blocks,
    pair_lists,
    batch_pairs,
):
    slot_count = points.shape[0]
    grid_size = points.shape[3]
    columns = lax.axis_size("blk")
    per_owner = pair_lists.shape[3]
    held_pairs = density_blocks.shape[0]
    block_size = density_blocks.shape[1]
    entries = columns * per_owner
    list_size = LIST
    basis_width = list_size * block_size
    batch_rank = lax.axis_index("batch")
    plan_rows = lax.dynamic_slice_in_dim(load_plan[0], batch_rank * slot_count, slot_count)
    stored = lax.all_gather(hartree[:, 0, :], "batch", axis=0, tiled=True)
    potential = stored[plan_rows]
    wanted = pair_lists[0, 0]
    asked_slots = lax.all_to_all(wanted, "blk", split_axis=0, concat_axis=0, tiled=True)
    owner_base = jnp.arange(entries, dtype=jnp.int32) // per_owner * held_pairs
    global_ids = owner_base + wanted.reshape(entries)
    blank_table = jnp.zeros((entries, block_size, block_size), jnp.bfloat16)
    piece = lax.all_gather(density_blocks, "blk", axis=0, tiled=True)
    inside = (global_ids >= 0) & (global_ids < piece.shape[0])
    chosen = piece[jnp.clip(global_ids, 0, piece.shape[0] - 1)]
    fetched = jnp.where(inside[:, None, None], chosen, blank_table)
    group_size = 4
    loop_turns = slot_count // group_size

    def take_rows(value, turn_index):
        return lax.dynamic_slice_in_dim(value, turn_index * group_size, group_size, 0)

    def integrate(partial_table, turn_index):
        basis = evaluate(
            take_rows(points, turn_index)[:, 0],
            take_rows(centers, turn_index)[:, 0],
            take_rows(exponents, turn_index)[:, 0],
            take_rows(angular, turn_index)[:, 0],
        )
        slot_refs = take_rows(batch_pairs, turn_index)[:, 0]
        blocks = fetched[slot_refs]
        sub_density = (
            blocks.reshape(group_size, list_size, list_size, block_size, block_size)
            .transpose(0, 1, 3, 2, 4)
            .reshape(group_size, basis_width, basis_width)
        )
        inner = jnp.einsum("gpm,gmn->gpn", basis, sub_density, preferred_element_type=jnp.float32)
        grid_rho = jnp.sum(inner * basis.astype(jnp.float32), axis=-1)
        effective = take_rows(potential, turn_index) + exchange_potential(grid_rho)
        weight_rows = take_rows(grid_weights, turn_index)[:, 0]
        scaled = ((weight_rows * effective)[..., None] * basis.astype(jnp.float32)).astype(
            jnp.bfloat16
        )
        full_blocks = jnp.einsum("gpm,gpn->gmn", basis, scaled, preferred_element_type=jnp.float32)
        contributions = (
            full_blocks.reshape(group_size, list_size, block_size, list_size, block_size)
            .transpose(0, 1, 3, 2, 4)
            .reshape(group_size * list_size * list_size, block_size, block_size)
        )
        partial_table = partial_table.at[slot_refs.reshape(-1)].add(contributions)
        return (partial_table, grid_rho)

    zero_table = jnp.zeros((entries, block_size, block_size), jnp.float32)
    partial_table, rho_groups = lax.scan(integrate, zero_table, jnp.arange(loop_turns))
    grid_rho = rho_groups.reshape(slot_count, grid_size)
    received = lax.all_to_all(
        partial_table.reshape(columns, per_owner, block_size, block_size),
        "blk",
        split_axis=0,
        concat_axis=0,
        tiled=True,
    )
    owned_sums = (
        jnp.zeros((held_pairs, block_size, block_size), jnp.float32)
        .at[asked_slots.reshape(entries)]
        .add(received.reshape(entries, block_size, block_size))
    )
    hamiltonian = lax.psum(owned_sums, "batch")
    batch_total = load_plan.shape[1]
    placement = (plan_rows[None, :] == jnp.arange(batch_total, dtype=jnp.int32)[:, None]).astype(
        jnp.float32
    )
    spread_rows = jnp.dot(
        placement, grid_rho, precision=lax.Precision.HIGHEST, preferred_element_type=jnp.float32
    )
    density = lax.psum_scatter(spread_rows, "batch", scatter_dimension=0, tiled=True)
    return (hamiltonian, density[:, None, :])


def solution(mesh):
    return jax.shard_map(
        on_device,
        mesh=mesh,
        in_specs=(
            P("batch", "blk", None, None),
            P("batch", "blk", None, None),
            P("batch", "blk", None),
            P("batch", "blk", None, None),
            P("batch", "blk", None),
            P("batch", "blk", None),
            P("blk", None),
            P("blk", None, None),
            P("batch", "blk", None, None),
            P("batch", "blk", None),
        ),
        out_specs=(P("blk", None, None), P("batch", "blk", None)),
        check_vma=False,
    )
```

profile of v0, /device:TPU:8, one launch (start us, length us, event | category | flops | bytes accessed | tf_op | source)
XLA Modules:
  0.0 800.7 jit_solution(2311108223574678586)
XLA Ops:
  10.7 9.1 %all-to-all-start = ((s32[16,1,2]{2,1,0:T(1,128)}), s32[16,1,2]{2,1,0:T(1,128)S(1)}, u32[]{:S(2)}, u32[]{:S(2)}) async-start(s32[16,1,2]{2,1,0:T(1,128)} %copy.56), calls=%async_computation | async-start | bytes 16384 | tf_op jit(solution)/shard_map/all_to_all | solution.py:51
  22.3 76.3 %all-gather.6.cloned.1.call-done = f32[1024,1,256]{2,0,1:T(8,128)} async-done(((f32[32,1,256]{2,0,1:T(8,128)}), f32[1024,1,256]{2,0,1:T(8,128)}) %all-gather.6.cloned.1.call-update) | async-done | bytes 1048592 | tf_op jit(solution)/shard_map/all_gather | solution.py:48
  98.6 1.8 gather_fusion.1
  100.4 54.4 %all-gather.4.cloned.1.call-done = bf16[256,128,128]{2,1,0:T(8,128)(2,1)} async-done(((bf16[16,128,128]{2,1,0:T(8,128)(2,1)}), bf16[256,128,128]{2,1,0:T(8,128)(2,1)}) %all-gather.4.cloned.1.call-update) | async-done | bytes 8388624 | tf_op jit(solution)/shard_map/all_gather | solution.py:55
  154.8 4.1 gather_fusion.2
  160.6 234.9 %while.12 = (s32[]{:T(128)}, f32[32,128,128]{2,1,0:T(8,128)}, f32[8,4,256]{2,1,0:T(4,128)S(1)}, s32[8]{0:T(128)S(1)}, s32[32,1,9]{2,0,1:T(8,128)S(1)}, /*index=5...) while((s32[]{:T(128)}, f32[32,128,128]{2,1,0:T(8,128)}, ...), condition=%wide.region_3.4_spmd, body=%wide.region_0.3_spmd.sunk | while | flops 633674496 | bytes 35997664 | solution.py:96
  167.2 2.9 fusion.49
  170.8 4.2 fusion.51
  175.1 3.5 reshape.302
  178.5 1.7 copy.100
  180.3 9.6 %scatter_fusion = f32[32,128,128]{2,1,0:T(8,128)} fusion(f32[32,128,128]{2,1,0:T(8,128)} %get-tuple-element.276, s32[36]{0:T(128)S(1)} %fusion.47, f32[36,128,128]{2,1,0:T(8,128)} %bitcast.106), kind=kCustom, calls=%fused_computation.3.clone.1 | custom fusion | flops 589824 | bytes 7078032 | tf_op jit(solution)/shard_map/while/body/eval_jaxpr/scatter-add | solution.py:92
  196.6 2.9 fusion.49
  200.2 4.2 fusion.51
  204.4 3.5 reshape.302
  207.9 1.7 copy.100
  209.7 9.7 %scatter_fusion = f32[32,128,128]{2,1,0:T(8,128)} fusion(f32[32,128,128]{2,1,0:T(8,128)} %get-tuple-element.276, s32[36]{0:T(128)S(1)} %fusion.47, f32[36,128,128]{2,1,0:T(8,128)} %bitcast.106), kind=kCustom, calls=%fused_computation.3.clone.1 | custom fusion | flops 589824 | bytes 7078032 | tf_op jit(solution)/shard_map/while/body/eval_jaxpr/scatter-add | solution.py:92
  226.0 2.9 fusion.49
  229.6 4.2 fusion.51
  233.8 3.5 reshape.302
  237.3 1.7 copy.100
  239.1 9.7 %scatter_fusion = f32[32,128,128]{2,1,0:T(8,128)} fusion(f32[32,128,128]{2,1,0:T(8,128)} %get-tuple-element.276, s32[36]{0:T(128)S(1)} %fusion.47, f32[36,128,128]{2,1,0:T(8,128)} %bitcast.106), kind=kCustom, calls=%fused_computation.3.clone.1 | custom fusion | flops 589824 | bytes 7078032 | tf_op jit(solution)/shard_map/while/body/eval_jaxpr/scatter-add | solution.py:92
  255.4 2.9 fusion.49
  259.0 4.2 fusion.51
  263.2 3.5 reshape.302
  266.7 1.7 copy.100
  268.5 9.7 %scatter_fusion = f32[32,128,128]{2,1,0:T(8,128)} fusion(f32[32,128,128]{2,1,0:T(8,128)} %get-tuple-element.276, s32[36]{0:T(128)S(1)} %fusion.47, f32[36,128,128]{2,1,0:T(8,128)} %bitcast.106), kind=kCustom, calls=%fused_computation.3.clone.1 | custom fusion | flops 589824 | bytes 7078032 | tf_op jit(solution)/shard_map/while/body/eval_jaxpr/scatter-add | solution.py:92
  284.8 2.9 fusion.49
  288.4 4.2 fusion.51
  292.6 3.5 reshape.302
  297.9 9.7 %scatter_fusion = f32[32,128,128]{2,1,0:T(8,128)} fusion(f32[32,128,128]{2,1,0:T(8,128)} %get-tuple-element.276, s32[36]{0:T(128)S(1)} %fusion.47, f32[36,128,128]{2,1,0:T(8,128)} %bitcast.106), kind=kCustom, calls=%fused_computation.3.clone.1 | custom fusion | flops 589824 | bytes 7078032 | tf_op jit(solution)/shard_map/while/body/eval_jaxpr/scatter-add | solution.py:92
  314.2 2.9 fusion.49
  317.8 4.2 fusion.51
  322.0 3.5 reshape.302
  327.3 9.6 %scatter_fusion = f32[32,128,128]{2,1,0:T(8,128)} fusion(f32[32,128,128]{2,1,0:T(8,128)} %get-tuple-element.276, s32[36]{0:T(128)S(1)} %fusion.47, f32[36,128,128]{2,1,0:T(8,128)} %bitcast.106), kind=kCustom, calls=%fused_computation.3.clone.1 | custom fusion | flops 589824 | bytes 7078032 | tf_op jit(solution)/shard_map/while/body/eval_jaxpr/scatter-add | solution.py:92
  343.5 2.9 fusion.49
  347.1 4.2 fusion.51
  351.3 3.5 reshape.302
  356.6 9.6 %scatter_fusion = f32[32,128,128]{2,1,0:T(8,128)} fusion(f32[32,128,128]{2,1,0:T(8,128)} %get-tuple-element.276, s32[36]{0:T(128)S(1)} %fusion.47, f32[36,128,128]{2,1,0:T(8,128)} %bitcast.106), kind=kCustom, calls=%fused_computation.3.clone.1 | custom fusion | flops 589824 | bytes 7078032 | tf_op jit(solution)/shard_map/while/body/eval_jaxpr/scatter-add | solution.py:92
  372.8 2.9 fusion.49
  376.5 4.2 fusion.51
  380.7 3.5 reshape.302
  386.0 9.6 %scatter_fusion = f32[32,128,128]{2,1,0:T(8,128)} fusion(f32[32,128,128]{2,1,0:T(8,128)} %get-tuple-element.276, s32[36]{0:T(128)S(1)} %fusion.47, f32[36,128,128]{2,1,0:T(8,128)} %bitcast.106), kind=kCustom, calls=%fused_computation.3.clone.1 | custom fusion | flops 589824 | bytes 7078032 | tf_op jit(solution)/shard_map/while/body/eval_jaxpr/scatter-add | solution.py:92
  395.5 6.8 all-to-all-start.1
  406.1 43.7 %all-to-all-done.1 = f32[16,2,128,128]{3,2,1,0:T(8,128)S(1)} async-done(((f32[16,2,128,128]{3,2,1,0:T(8,128)}), f32[16,2,128,128]{3,2,1,0:T(8,128)S(1)}, u32[]{:S(2)}, u32[]{:S(2)}) %all-to-all-start.1) | async-done | bytes 2097184 | tf_op jit(solution)/shard_map/all_to_all | solution.py:98
  449.9 2.7 scatter_fusion.1
  453.5 175.6 %reduce-scatter.2.cloned.1.call-done = f32[32,256]{1,0:T(8,128)} async-done(((f32[1024,256]{1,0:T(8,128)}), f32[32,256]{1,0:T(8,128)}) %reduce-scatter.2.cloned.1.call-update) | async-done | bytes 32784 | tf_op jit(solution)/shard_map/reduce_scatter | solution.py:118
  630.5 161.3 %all-reduce.2.cloned.1.call-done = f32[16,128,128]{2,1,0:T(8,128)} async-done(((f32[16,128,128]{2,1,0:T(8,128)}), f32[16,128,128]{2,1,0:T(8,128)}) %all-reduce.2.cloned.1.call-update) | async-done | bytes 1048592 | tf_op jit(solution)/shard_map/psum | solution.py:110
  791.8 2.3 copy.114
  (247 shorter events, 74.0 us)
Async XLA Ops:
  7.2 91.4 %all-gather.6.cloned.1.call-start = ((), (), s32[]{:S(2)}) async-start(), calls=%async_computation.6 | async-start | bytes 1081344 | tf_op jit(solution)/shard_map/all_gather | solution.py:48
  8.6 146.2 %all-gather.4.cloned.1.call-start = ((), (), s32[]{:S(2)}) async-start(), calls=%async_computation.3 | async-start | bytes 8912896 | tf_op jit(solution)/shard_map/all_gather | solution.py:55
  10.7 384.8 %all-to-all-start = ((s32[16,1,2]{2,1,0:T(1,128)}), s32[16,1,2]{2,1,0:T(1,128)S(1)}, u32[]{:S(2)}, u32[]{:S(2)}) async-start(s32[16,1,2]{2,1,0:T(1,128)} %copy.56), calls=%async_computation | async-start | bytes 16384 | tf_op jit(solution)/shard_map/all_to_all | solution.py:51
  160.6 3.8 copy-start
  180.3 9.6 %copy-start.1 = (bf16[32,128,128]{2,1,0:T(8,128)(2,1)S(1)}, bf16[32,128,128]{2,1,0:T(8,128)(2,1)}, u32[]{:S(2)}) copy-start(bf16[32,128,128]{2,1,0:T(8,128)(2,1)} %copy-done) | copy-start | bytes 3145732 | tf_op jit(solution)/shard_map/while
  190.0 3.8 copy-start
  209.7 9.7 %copy-start.1 = (bf16[32,128,128]{2,1,0:T(8,128)(2,1)S(1)}, bf16[32,128,128]{2,1,0:T(8,128)(2,1)}, u32[]{:S(2)}) copy-start(bf16[32,128,128]{2,1,0:T(8,128)(2,1)} %copy-done) | copy-start | bytes 3145732 | tf_op jit(solution)/shard_map/while
  219.4 3.8 copy-start
  239.1 9.7 %copy-start.1 = (bf16[32,128,128]{2,1,0:T(8,128)(2,1)S(1)}, bf16[32,128,128]{2,1,0:T(8,128)(2,1)}, u32[]{:S(2)}) copy-start(bf16[32,128,128]{2,1,0:T(8,128)(2,1)} %copy-done) | copy-start | bytes 3145732 | tf_op jit(solution)/shard_map/while
  248.8 3.8 copy-start
  268.5 9.8 %copy-start.1 = (bf16[32,128,128]{2,1,0:T(8,128)(2,1)S(1)}, bf16[32,128,128]{2,1,0:T(8,128)(2,1)}, u32[]{:S(2)}) copy-start(bf16[32,128,128]{2,1,0:T(8,128)(2,1)} %copy-done) | copy-start | bytes 3145732 | tf_op jit(solution)/shard_map/while
  278.2 3.8 copy-start
  297.9 9.7 %copy-start.1 = (bf16[32,128,128]{2,1,0:T(8,128)(2,1)S(1)}, bf16[32,128,128]{2,1,0:T(8,128)(2,1)}, u32[]{:S(2)}) copy-start(bf16[32,128,128]{2,1,0:T(8,128)(2,1)} %copy-done) | copy-start | bytes 3145732 | tf_op jit(solution)/shard_map/while
  307.6 3.8 copy-start
  327.3 9.6 %copy-start.1 = (bf16[32,128,128]{2,1,0:T(8,128)(2,1)S(1)}, bf16[32,128,128]{2,1,0:T(8,128)(2,1)}, u32[]{:S(2)}) copy-start(bf16[32,128,128]{2,1,0:T(8,128)(2,1)} %copy-done) | copy-start | bytes 3145732 | tf_op jit(solution)/shard_map/while
  336.9 3.8 copy-start
  356.6 9.6 %copy-start.1 = (bf16[32,128,128]{2,1,0:T(8,128)(2,1)S(1)}, bf16[32,128,128]{2,1,0:T(8,128)(2,1)}, u32[]{:S(2)}) copy-start(bf16[32,128,128]{2,1,0:T(8,128)(2,1)} %copy-done) | copy-start | bytes 3145732 | tf_op jit(solution)/shard_map/while
  366.3 3.8 copy-start
  386.0 9.6 %copy-start.1 = (bf16[32,128,128]{2,1,0:T(8,128)(2,1)S(1)}, bf16[32,128,128]{2,1,0:T(8,128)(2,1)}, u32[]{:S(2)}) copy-start(bf16[32,128,128]{2,1,0:T(8,128)(2,1)} %copy-done) | copy-start | bytes 3145732 | tf_op jit(solution)/shard_map/while
  395.5 54.2 %all-to-all-start.1 = ((f32[16,2,128,128]{3,2,1,0:T(8,128)}), f32[16,2,128,128]{3,2,1,0:T(8,128)S(1)}, u32[]{:S(2)}, u32[]{:S(2)}) async-start(f32[16,2,128,128]{3,2,1,0:T(8,128)} %bitcast.108), calls=%async_computation.1 | async-start | bytes 4194304 | tf_op jit(solution)/shard_map/all_to_all | solution.py:98
  402.4 226.8 %reduce-scatter.2.cloned.1.call-start = ((), (), s32[]{:S(2)}) async-start(), calls=%async_computation.5 | async-start | bytes 1081344 | tf_op jit(solution)/shard_map/reduce_scatter | solution.py:118
  404.7 387.1 %all-reduce.2.cloned.1.call-start = ((), (), s32[]{:S(2)}) async-start(), calls=%async_computation.4 | async-start | bytes 2097152 | tf_op jit(solution)/shard_map/psum | solution.py:110
  452.5 1.0 copy-start.2
Sparse Core Ops, SparseCore 0:
  11.7 86.7 all-gather.5
  100.7 54.0 all-gather.3
  407.6 221.4 reduce-scatter.1
  633.0 158.7 all-reduce.1
where the time goes:
time: 804 us; the launch traced here: 801 us
  waiting for transfers between devices  512 us (64%)
  local copies, waits for them, and re-layouts  112 us (14%)
  other arithmetic  81.9 us (10%)
  matrix products  58.4 us (7%)
  starting transfers between devices  16.1 us (2%)
  between operations  13.9 us (2%)
    reduce_scatter x1, waiting for transfers between devices, on_device(): lax.psum_scatter(spread_rows, 'batch', scatter_dimension=0, tiled=True)  176 us
    psum x1, waiting for transfers between devices, on_device(): hamiltonian = lax.psum(owned_sums, 'batch')  161 us
    scatter-add x8, other arithmetic, integrate(): partial_table = partial_table.at[slot_refs.reshape(-1)].add(contributions)  77.2 us
    all_gather x1, waiting for transfers between devices, on_device(): stored = lax.all_gather(hartree[:, 0, :], 'batch', axis=0, tiled=True)  76.3 us
    all_gather x1, waiting for transfers between devices, on_device(): piece = lax.all_gather(density_blocks, 'blk', axis=0, tiled=True)  54.4 us
    all_to_all x1, waiting for transfers between devices, on_device(): lax.all_to_all(partial_table.reshape(columns, per_owner, block_size, bloc...  43.7 us
    dot_general x8, matrix products, integrate(): jnp.einsum('gpm,gpn->gmn', basis, scaled, preferred_element_type=jnp.floa...  33.7 us
    reshape x8, local copies, waits for them, and re-layouts, integrate(): full_blocks.reshape(group_size, list_size, block_size, list_size, block_s...  27.7 us
  transfers between devices with their start and end apart: 6, of which 5 were waited for; matrix products, arithmetic and copies ran while one was open for 31% of the time, Pallas kernels for 0%

commit v1 on v0

--- a/solution.py
+++ b/solution.py
@@ -52,7 +52,12 @@
     owner_base = jnp.arange(entries, dtype=jnp.int32) // per_owner * held_pairs
     global_ids = owner_base + wanted.reshape(entries)
     blank_table = jnp.zeros((entries, block_size, block_size), jnp.bfloat16)
-    piece = lax.all_gather(density_blocks, "blk", axis=0, tiled=True)
+    ring = [density_blocks]
+    for hop in range(15):
+        ring.append(lax.ppermute(ring[-1], "blk", [(dev, (dev + 1) % 16) for dev in range(16)]))
+    piece = jnp.roll(
+        jnp.concatenate(ring[::-1], axis=0), (lax.axis_index("blk") + 1) * ring[0].shape[0], axis=0
+    )
     inside = (global_ids >= 0) & (global_ids < piece.shape[0])
     chosen = piece[jnp.clip(global_ids, 0, piece.shape[0] - 1)]
     fetched = jnp.where(inside[:, None, None], chosen, blank_table)

time: 804 us -> 905 us (1.13)
  local copies, waits for them, and re-layouts: 112 us -> 164 us
  waiting for transfers between devices: 512 us -> 553 us
    ppermute x0 -> x15, waiting for transfers between devices: none -> 122 us  [on_device(): lax.ppermute(ring[-1], 'blk', [(dev, (dev + 1) % 16) for dev in range(16)])]
    all_gather x1 -> x0, waiting for transfers between devices: 54.4 us -> none  [on_device(): piece = lax.all_gather(density_blocks, 'blk', axis=0, tiled=True)]
    unnamed x6 -> x55, local copies, waits for them, and re-layouts: 6.79 us -> 47 us
    all_gather x1, waiting for transfers between devices: 76.3 us -> 54.3 us  [on_device(): stored = lax.all_gather(hartree[:, 0, :], 'batch', axis=0, tiled=True)]
    dynamic_slice x0 -> x1, local copies, waits for them, and re-layouts: none -> 10.4 us  [on_device(): jnp.roll(jnp.concatenate(ring[::-1], axis=0), (lax.axis_index('blk') + 1)...]
  transfers between devices with their start and end apart: 6 -> 20, of which waited for: 5 -> 17; matrix products, arithmetic and copies ran while one was open for 31% -> 33% of each run, Pallas kernels for 0% -> 0%
where the time goes in v1:
time: 905 us; the launch traced here: 901 us
  waiting for transfers between devices  553 us (61%)
  local copies, waits for them, and re-layouts  164 us (18%)
  other arithmetic  82.4 us (9%)
  matrix products  58.5 us (6%)
  starting transfers between devices  23 us (3%)
  between operations  13.9 us (2%)
    reduce_scatter x1, waiting for transfers between devices, on_device(): lax.psum_scatter(spread_rows, 'batch', scatter_dimension=0, tiled=True)  172 us
    psum x1, waiting for transfers between devices, on_device(): hamiltonian = lax.psum(owned_sums, 'batch')  161 us
    ppermute x15, waiting for transfers between devices, on_device(): lax.ppermute(ring[-1], 'blk', [(dev, (dev + 1) % 16) for dev in range(16)])  122 us
    scatter-add x8, other arithmetic, integrate(): partial_table = partial_table.at[slot_refs.reshape(-1)].add(contributions)  77.7 us
    all_gather x1, waiting for transfers between devices, on_device(): stored = lax.all_gather(hartree[:, 0, :], 'batch', axis=0, tiled=True)  54.3 us
    unnamed x55, local copies, waits for them, and re-layouts  47 us
    all_to_all x1, waiting for transfers between devices, on_device(): lax.all_to_all(partial_table.reshape(columns, per_owner, block_size, bloc...  43.7 us
    dot_general x8, matrix products, integrate(): jnp.einsum('gpm,gpn->gmn', basis, scaled, preferred_element_type=jnp.floa...  33.7 us
  transfers between devices with their start and end apart: 20, of which 17 were waited for; matrix products, arithmetic and copies ran while one was open for 33% of the time, Pallas kernels for 0%

profile of v1, /device:TPU:8, one launch (start us, length us, event | category | flops | bytes accessed | tf_op | source)
XLA Modules:
  0.0 900.9 jit_solution(5807696902400815685)
XLA Ops:
  7.2 8.8 collective-permute-done
  16.0 8.6 collective-permute-done.1
  24.6 8.6 collective-permute-done.2
  33.3 8.6 collective-permute-done.3
  41.9 9.2 %collective-permute-done.4 = bf16[16,128,128]{2,1,0:T(8,128)(2,1)S(1)} collective-permute-done((bf16[16,128,128]{2,1,0:T(8,128)(2,1)S(1)}, bf16[16,128,128]{2,1,0:T(8,128)(2,1)S(1)}, u32[]{:S(2)}, u32[]{:S(2)}) %collective-permute-start.4) | collective-permute-done | bytes 524320 | tf_op jit(solution)/shard_map/ppermute | solution.py:57
  51.1 9.8 %collective-permute-done.5 = bf16[16,128,128]{2,1,0:T(8,128)(2,1)S(1)} collective-permute-done((bf16[16,128,128]{2,1,0:T(8,128)(2,1)S(1)}, bf16[16,128,128]{2,1,0:T(8,128)(2,1)S(1)}, u32[]{:S(2)}, u32[]{:S(2)}) %collective-permute-start.5) | collective-permute-done | bytes 524320 | tf_op jit(solution)/shard_map/ppermute | solution.py:57
  60.9 9.8 %collective-permute-done.6 = bf16[16,128,128]{2,1,0:T(8,128)(2,1)S(1)} collective-permute-done((bf16[16,128,128]{2,1,0:T(8,128)(2,1)S(1)}, bf16[16,128,128]{2,1,0:T(8,128)(2,1)S(1)}, u32[]{:S(2)}, u32[]{:S(2)}) %collective-permute-start.6) | collective-permute-done | bytes 524320 | tf_op jit(solution)/shard_map/ppermute | solution.py:57
  71.5 9.8 %collective-permute-done.7 = bf16[16,128,128]{2,1,0:T(8,128)(2,1)S(1)} collective-permute-done((bf16[16,128,128]{2,1,0:T(8,128)(2,1)S(1)}, bf16[16,128,128]{2,1,0:T(8,128)(2,1)S(1)}, u32[]{:S(2)}, u32[]{:S(2)}) %collective-permute-start.7) | collective-permute-done | bytes 524320 | tf_op jit(solution)/shard_map/ppermute | solution.py:57
  82.2 9.8 %collective-permute-done.8 = bf16[16,128,128]{2,1,0:T(8,128)(2,1)S(1)} collective-permute-done((bf16[16,128,128]{2,1,0:T(8,128)(2,1)S(1)}, bf16[16,128,128]{2,1,0:T(8,128)(2,1)S(1)}, u32[]{:S(2)}, u32[]{:S(2)}) %collective-permute-start.8) | collective-permute-done | bytes 524320 | tf_op jit(solution)/shard_map/ppermute | solution.py:57
  92.8 9.8 %collective-permute-done.9 = bf16[16,128,128]{2,1,0:T(8,128)(2,1)S(1)} collective-permute-done((bf16[16,128,128]{2,1,0:T(8,128)(2,1)S(1)}, bf16[16,128,128]{2,1,0:T(8,128)(2,1)S(1)}, u32[]{:S(2)}, u32[]{:S(2)}) %collective-permute-start.9) | collective-permute-done | bytes 524320 | tf_op jit(solution)/shard_map/ppermute | solution.py:57
  103.4 9.9 %collective-permute-done.10 = bf16[16,128,128]{2,1,0:T(8,128)(2,1)} collective-permute-done((bf16[16,128,128]{2,1,0:T(8,128)(2,1)S(1)}, bf16[16,128,128]{2,1,0:T(8,128)(2,1)}, u32[]{:S(2)}, u32[]{:S(2)}) %collective-permute-start.10) | collective-permute-done | bytes 524320 | tf_op jit(solution)/shard_map/ppermute | solution.py:57
  114.7 8.8 collective-permute-done.11
  123.5 10.1 %collective-permute-done.12 = bf16[16,128,128]{2,1,0:T(8,128)(2,1)} collective-permute-done((bf16[16,128,128]{2,1,0:T(8,128)(2,1)}, bf16[16,128,128]{2,1,0:T(8,128)(2,1)}, u32[]{:S(2)}, u32[]{:S(2)}) %collective-permute-start.12) | collective-permute-done | bytes 524320 | tf_op jit(solution)/shard_map/ppermute | solution.py:57
  134.9 15.5 %all-to-all-start = ((s32[16,1,2]{2,1,0:T(1,128)}), s32[16,1,2]{2,1,0:T(1,128)S(1)}, u32[]{:S(2)}, u32[]{:S(2)}) async-start(s32[16,1,2]{2,1,0:T(1,128)} %copy.56), calls=%async_computation | async-start | bytes 16384 | tf_op jit(solution)/shard_map/all_to_all | solution.py:51
  153.1 54.3 %all-gather.3.cloned.1.call-done = f32[1024,1,256]{2,0,1:T(8,128)} async-done(((f32[32,1,256]{2,0,1:T(8,128)}), f32[1024,1,256]{2,0,1:T(8,128)}) %all-gather.3.cloned.1.call-update) | async-done | bytes 1048592 | tf_op jit(solution)/shard_map/all_gather | solution.py:48
  247.1 10.4 %constant_dynamic-slice_fusion.6 = bf16[256,128,128]{2,1,0:T(8,128)(2,1)} fusion(bf16[512,128,128]{2,1,0:T(8,128)(2,1)} %constant_dynamic-update-slice_fusion, s32[]{:T(128)S(6)} %select_n.102), kind=kLoop, calls=%fused_computation.114 | loop fusion | bytes 16777220 | tf_op jit(solution)/shard_map/jit(_roll_dynamic)/dynamic_slice | solution.py:58
  257.5 4.1 gather_fusion.2
  263.4 235.6 %while.12 = (s32[]{:T(128)}, f32[32,128,128]{2,1,0:T(8,128)}, f32[8,4,256]{2,1,0:T(4,128)S(1)}, s32[8]{0:T(128)S(1)}, s32[32,1,9]{2,0,1:T(8,128)S(1)}, /*index=5...) while((s32[]{:T(128)}, f32[32,128,128]{2,1,0:T(8,128)}, ...), condition=%wide.region_3.4_spmd, body=%wide.region_0.3_spmd.sunk | while | flops 633674496 | bytes 35997664 | solution.py:101
  273.6 4.2 fusion.51
  277.8 3.5 reshape.302
  283.1 9.7 %scatter_fusion = f32[32,128,128]{2,1,0:T(8,128)} fusion(f32[32,128,128]{2,1,0:T(8,128)} %get-tuple-element.276, s32[36]{0:T(128)S(1)} %fusion.47, f32[36,128,128]{2,1,0:T(8,128)} %bitcast.106), kind=kCustom, calls=%fused_computation.3.clone.1 | custom fusion | flops 589824 | bytes 7078032 | tf_op jit(solution)/shard_map/while/body/eval_jaxpr/scatter-add | solution.py:97
  303.0 4.2 fusion.51
  307.2 3.5 reshape.302
  312.5 9.7 %scatter_fusion = f32[32,128,128]{2,1,0:T(8,128)} fusion(f32[32,128,128]{2,1,0:T(8,128)} %get-tuple-element.276, s32[36]{0:T(128)S(1)} %fusion.47, f32[36,128,128]{2,1,0:T(8,128)} %bitcast.106), kind=kCustom, calls=%fused_computation.3.clone.1 | custom fusion | flops 589824 | bytes 7078032 | tf_op jit(solution)/shard_map/while/body/eval_jaxpr/scatter-add | solution.py:97
  328.8 2.9 fusion.49
  332.5 4.2 fusion.51
  336.7 3.5 reshape.302
  342.0 9.7 %scatter_fusion = f32[32,128,128]{2,1,0:T(8,128)} fusion(f32[32,128,128]{2,1,0:T(8,128)} %get-tuple-element.276, s32[36]{0:T(128)S(1)} %fusion.47, f32[36,128,128]{2,1,0:T(8,128)} %bitcast.106), kind=kCustom, calls=%fused_computation.3.clone.1 | custom fusion | flops 589824 | bytes 7078032 | tf_op jit(solution)/shard_map/while/body/eval_jaxpr/scatter-add | solution.py:97
  361.9 4.2 fusion.51
  366.1 3.5 reshape.302
  371.4 9.8 %scatter_fusion = f32[32,128,128]{2,1,0:T(8,128)} fusion(f32[32,128,128]{2,1,0:T(8,128)} %get-tuple-element.276, s32[36]{0:T(128)S(1)} %fusion.47, f32[36,128,128]{2,1,0:T(8,128)} %bitcast.106), kind=kCustom, calls=%fused_computation.3.clone.1 | custom fusion | flops 589824 | bytes 7078032 | tf_op jit(solution)/shard_map/while/body/eval_jaxpr/scatter-add | solution.py:97
  391.5 4.2 fusion.51
  395.7 3.5 reshape.302
  401.0 9.7 %scatter_fusion = f32[32,128,128]{2,1,0:T(8,128)} fusion(f32[32,128,128]{2,1,0:T(8,128)} %get-tuple-element.276, s32[36]{0:T(128)S(1)} %fusion.47, f32[36,128,128]{2,1,0:T(8,128)} %bitcast.106), kind=kCustom, calls=%fused_computation.3.clone.1 | custom fusion | flops 589824 | bytes 7078032 | tf_op jit(solution)/shard_map/while/body/eval_jaxpr/scatter-add | solution.py:97
  417.3 2.9 fusion.49
  420.9 4.2 fusion.51
  425.1 3.5 reshape.302
  430.4 9.6 %scatter_fusion = f32[32,128,128]{2,1,0:T(8,128)} fusion(f32[32,128,128]{2,1,0:T(8,128)} %get-tuple-element.276, s32[36]{0:T(128)S(1)} %fusion.47, f32[36,128,128]{2,1,0:T(8,128)} %bitcast.106), kind=kCustom, calls=%fused_computation.3.clone.1 | custom fusion | flops 589824 | bytes 7078032 | tf_op jit(solution)/shard_map/while/body/eval_jaxpr/scatter-add | solution.py:97
  450.3 4.2 fusion.51
  454.5 3.5 reshape.302
  459.8 9.8 %scatter_fusion = f32[32,128,128]{2,1,0:T(8,128)} fusion(f32[32,128,128]{2,1,0:T(8,128)} %get-tuple-element.276, s32[36]{0:T(128)S(1)} %fusion.47, f32[36,128,128]{2,1,0:T(8,128)} %bitcast.106), kind=kCustom, calls=%fused_computation.3.clone.1 | custom fusion | flops 589824 | bytes 7078032 | tf_op jit(solution)/shard_map/while/body/eval_jaxpr/scatter-add | solution.py:97
  479.8 4.2 fusion.51
  484.0 3.5 reshape.302
  489.3 9.7 %scatter_fusion = f32[32,128,128]{2,1,0:T(8,128)} fusion(f32[32,128,128]{2,1,0:T(8,128)} %get-tuple-element.276, s32[36]{0:T(128)S(1)} %fusion.47, f32[36,128,128]{2,1,0:T(8,128)} %bitcast.106), kind=kCustom, calls=%fused_computation.3.clone.1 | custom fusion | flops 589824 | bytes 7078032 | tf_op jit(solution)/shard_map/while/body/eval_jaxpr/scatter-add | solution.py:97
  499.0 7.2 all-to-all-start.1
  509.9 43.7 %all-to-all-done.1 = f32[16,2,128,128]{3,2,1,0:T(8,128)S(1)} async-done(((f32[16,2,128,128]{3,2,1,0:T(8,128)}), f32[16,2,128,128]{3,2,1,0:T(8,128)S(1)}, u32[]{:S(2)}, u32[]{:S(2)}) %all-to-all-start.1) | async-done | bytes 2097184 | tf_op jit(solution)/shard_map/all_to_all | solution.py:103
  557.3 171.9 %reduce-scatter.2.cloned.1.call-done = f32[32,256]{1,0:T(8,128)} async-done(((f32[1024,256]{1,0:T(8,128)}), f32[32,256]{1,0:T(8,128)}) %reduce-scatter.2.cloned.1.call-update) | async-done | bytes 32784 | tf_op jit(solution)/shard_map/reduce_scatter | solution.py:123
  730.7 161.4 %all-reduce.2.cloned.1.call-done = f32[16,128,128]{2,1,0:T(8,128)} async-done(((f32[16,128,128]{2,1,0:T(8,128)}), f32[16,128,128]{2,1,0:T(8,128)}) %all-reduce.2.cloned.1.call-update) | async-done | bytes 1048592 | tf_op jit(solution)/shard_map/psum | solution.py:115
  (325 shorter events, 145.8 us)
Async XLA Ops:
  7.2 200.3 %all-gather.3.cloned.1.call-start = ((), (), s32[]{:S(2)}) async-start(), calls=%async_computation.5 | async-start | bytes 1081344 | tf_op jit(solution)/shard_map/all_gather | solution.py:48
  7.2 8.8 collective-permute-start
  16.0 8.6 collective-permute-start.1
  24.6 8.6 collective-permute-start.2
  33.3 8.6 collective-permute-start.3
  41.9 9.2 %collective-permute-start.4 = (bf16[16,128,128]{2,1,0:T(8,128)(2,1)S(1)}, bf16[16,128,128]{2,1,0:T(8,128)(2,1)S(1)}, u32[]{:S(2)}, u32[]{:S(2)}) collective-permute-start(bf16[16,128,128]{2,1,0:T(8,128)(2,1)S(1)} %collective-permute-done.3), channel_id=1, source_target_pairs={{0,1},{1,2},{2,3},{3,4},{4,5},{5,6},{6,7},{7,8},{8,9},{9,10},{10,1... | collective-permute-start | bytes 1572872 | tf_op jit(solution)/shard_map/ppermute | solution.py:57
  51.1 9.8 %collective-permute-start.5 = (bf16[16,128,128]{2,1,0:T(8,128)(2,1)S(1)}, bf16[16,128,128]{2,1,0:T(8,128)(2,1)S(1)}, u32[]{:S(2)}, u32[]{:S(2)}) collective-permute-start(bf16[16,128,128]{2,1,0:T(8,128)(2,1)S(1)} %collective-permute-done.4), channel_id=1, source_target_pairs={{0,1},{1,2},{2,3},{3,4},{4,5},{5,6},{6,7},{7,8},{8,9},{9,10},{10,1... | collective-permute-start | bytes 1572872 | tf_op jit(solution)/shard_map/ppermute | solution.py:57
  60.9 9.8 %collective-permute-start.6 = (bf16[16,128,128]{2,1,0:T(8,128)(2,1)S(1)}, bf16[16,128,128]{2,1,0:T(8,128)(2,1)S(1)}, u32[]{:S(2)}, u32[]{:S(2)}) collective-permute-start(bf16[16,128,128]{2,1,0:T(8,128)(2,1)S(1)} %collective-permute-done.5), channel_id=1, source_target_pairs={{0,1},{1,2},{2,3},{3,4},{4,5},{5,6},{6,7},{7,8},{8,9},{9,10},{10,1... | collective-permute-start | bytes 1572872 | tf_op jit(solution)/shard_map/ppermute | solution.py:57
  70.7 0.8 copy-start.4
  71.5 9.8 %collective-permute-start.7 = (bf16[16,128,128]{2,1,0:T(8,128)(2,1)S(1)}, bf16[16,128,128]{2,1,0:T(8,128)(2,1)S(1)}, u32[]{:S(2)}, u32[]{:S(2)}) collective-permute-start(bf16[16,128,128]{2,1,0:T(8,128)(2,1)S(1)} %collective-permute-done.6), channel_id=1, source_target_pairs={{0,1},{1,2},{2,3},{3,4},{4,5},{5,6},{6,7},{7,8},{8,9},{9,10},{10,1... | collective-permute-start | bytes 1572872 | tf_op jit(solution)/shard_map/ppermute | solution.py:57
  81.3 0.8 copy-start.6
  82.2 9.8 %collective-permute-start.8 = (bf16[16,128,128]{2,1,0:T(8,128)(2,1)S(1)}, bf16[16,128,128]{2,1,0:T(8,128)(2,1)S(1)}, u32[]{:S(2)}, u32[]{:S(2)}) collective-permute-start(bf16[16,128,128]{2,1,0:T(8,128)(2,1)S(1)} %collective-permute-done.7), channel_id=1, source_target_pairs={{0,1},{1,2},{2,3},{3,4},{4,5},{5,6},{6,7},{7,8},{8,9},{9,10},{10,1... | collective-permute-start | bytes 1572872 | tf_op jit(solution)/shard_map/ppermute | solution.py:57
  92.0 0.8 copy-start.8
  92.8 9.8 %collective-permute-start.9 = (bf16[16,128,128]{2,1,0:T(8,128)(2,1)S(1)}, bf16[16,128,128]{2,1,0:T(8,128)(2,1)S(1)}, u32[]{:S(2)}, u32[]{:S(2)}) collective-permute-start(bf16[16,128,128]{2,1,0:T(8,128)(2,1)S(1)} %collective-permute-done.8), channel_id=1, source_target_pairs={{0,1},{1,2},{2,3},{3,4},{4,5},{5,6},{6,7},{7,8},{8,9},{9,10},{10,1... | collective-permute-start | bytes 1572872 | tf_op jit(solution)/shard_map/ppermute | solution.py:57
  102.6 0.8 copy-start.10
  103.4 9.9 %collective-permute-start.10 = (bf16[16,128,128]{2,1,0:T(8,128)(2,1)S(1)}, bf16[16,128,128]{2,1,0:T(8,128)(2,1)}, u32[]{:S(2)}, u32[]{:S(2)}) collective-permute-start(bf16[16,128,128]{2,1,0:T(8,128)(2,1)S(1)} %collective-permute-done.9), channel_id=1, source_target_pairs={{0,1},{1,2},{2,3},{3,4},{4,5},{5,6},{6,7},{7,8},{8,9},{9,10},{10,1... | collective-permute-start | bytes 1572872 | tf_op jit(solution)/shard_map/ppermute | solution.py:57
  113.3 10.2 %collective-permute-start.11 = (bf16[16,128,128]{2,1,0:T(8,128)(2,1)}, bf16[16,128,128]{2,1,0:T(8,128)(2,1)}, u32[]{:S(2)}, u32[]{:S(2)}) collective-permute-start(bf16[16,128,128]{2,1,0:T(8,128)(2,1)} %collective-permute-done.10), channel_id=1, source_target_pairs={{0,1},{1,2},{2,3},{3,4},{4,5},{5,6},{6,7},{7,8},{8,9},{9,10},{10,1... | collective-permute-start | bytes 1572872 | tf_op jit(solution)/shard_map/ppermute | solution.py:57
  123.5 10.1 %collective-permute-start.12 = (bf16[16,128,128]{2,1,0:T(8,128)(2,1)}, bf16[16,128,128]{2,1,0:T(8,128)(2,1)}, u32[]{:S(2)}, u32[]{:S(2)}) collective-permute-start(bf16[16,128,128]{2,1,0:T(8,128)(2,1)} %collective-permute-done.11), channel_id=1, source_target_pairs={{0,1},{1,2},{2,3},{3,4},{4,5},{5,6},{6,7},{7,8},{8,9},{9,10},{10,1... | collective-permute-start | bytes 1572872 | tf_op jit(solution)/shard_map/ppermute | solution.py:57
  133.6 18.6 %collective-permute-start.13 = (bf16[16,128,128]{2,1,0:T(8,128)(2,1)}, bf16[16,128,128]{2,1,0:T(8,128)(2,1)}, u32[]{:S(2)}, u32[]{:S(2)}) collective-permute-start(bf16[16,128,128]{2,1,0:T(8,128)(2,1)} %collective-permute-done.12), channel_id=1, source_target_pairs={{0,1},{1,2},{2,3},{3,4},{4,5},{5,6},{6,7},{7,8},{8,9},{9,10},{10,1... | collective-permute-start | bytes 1572872 | tf_op jit(solution)/shard_map/ppermute | solution.py:57
  134.9 364.0 %all-to-all-start = ((s32[16,1,2]{2,1,0:T(1,128)}), s32[16,1,2]{2,1,0:T(1,128)S(1)}, u32[]{:S(2)}, u32[]{:S(2)}) async-start(s32[16,1,2]{2,1,0:T(1,128)} %copy.56), calls=%async_computation | async-start | bytes 16384 | tf_op jit(solution)/shard_map/all_to_all | solution.py:51
  152.2 57.1 %collective-permute-start.14 = (bf16[16,128,128]{2,1,0:T(8,128)(2,1)}, bf16[16,128,128]{2,1,0:T(8,128)(2,1)}, u32[]{:S(2)}, u32[]{:S(2)}) collective-permute-start(bf16[16,128,128]{2,1,0:T(8,128)(2,1)} %collective-permute-done.13), channel_id=1, source_target_pairs={{0,1},{1,2},{2,3},{3,4},{4,5},{5,6},{6,7},{7,8},{8,9},{9,10},{10,1... | collective-permute-start | bytes 1572872 | tf_op jit(solution)/shard_map/ppermute | solution.py:57
  213.1 5.8 copy-start.11
  215.0 4.8 copy-start.9
  217.0 3.7 copy-start.7
  218.9 2.5 copy-start.5
  224.8 2.5 copy-start.3
  263.4 3.8 copy-start
  283.1 9.7 %copy-start.1 = (bf16[32,128,128]{2,1,0:T(8,128)(2,1)S(1)}, bf16[32,128,128]{2,1,0:T(8,128)(2,1)}, u32[]{:S(2)}) copy-start(bf16[32,128,128]{2,1,0:T(8,128)(2,1)} %copy-done) | copy-start | bytes 3145732 | tf_op jit(solution)/shard_map/while
  292.8 3.8 copy-start
  312.5 9.8 %copy-start.1 = (bf16[32,128,128]{2,1,0:T(8,128)(2,1)S(1)}, bf16[32,128,128]{2,1,0:T(8,128)(2,1)}, u32[]{:S(2)}) copy-start(bf16[32,128,128]{2,1,0:T(8,128)(2,1)} %copy-done) | copy-start | bytes 3145732 | tf_op jit(solution)/shard_map/while
  322.3 3.8 copy-start
  342.0 9.7 %copy-start.1 = (bf16[32,128,128]{2,1,0:T(8,128)(2,1)S(1)}, bf16[32,128,128]{2,1,0:T(8,128)(2,1)}, u32[]{:S(2)}) copy-start(bf16[32,128,128]{2,1,0:T(8,128)(2,1)} %copy-done) | copy-start | bytes 3145732 | tf_op jit(solution)/shard_map/while
  351.7 3.8 copy-start
  371.4 9.8 %copy-start.1 = (bf16[32,128,128]{2,1,0:T(8,128)(2,1)S(1)}, bf16[32,128,128]{2,1,0:T(8,128)(2,1)}, u32[]{:S(2)}) copy-start(bf16[32,128,128]{2,1,0:T(8,128)(2,1)} %copy-done) | copy-start | bytes 3145732 | tf_op jit(solution)/shard_map/while
  381.3 3.8 copy-start
  401.0 9.7 %copy-start.1 = (bf16[32,128,128]{2,1,0:T(8,128)(2,1)S(1)}, bf16[32,128,128]{2,1,0:T(8,128)(2,1)}, u32[]{:S(2)}) copy-start(bf16[32,128,128]{2,1,0:T(8,128)(2,1)} %copy-done) | copy-start | bytes 3145732 | tf_op jit(solution)/shard_map/while
  410.7 3.8 copy-start
  430.4 9.7 %copy-start.1 = (bf16[32,128,128]{2,1,0:T(8,128)(2,1)S(1)}, bf16[32,128,128]{2,1,0:T(8,128)(2,1)}, u32[]{:S(2)}) copy-start(bf16[32,128,128]{2,1,0:T(8,128)(2,1)} %copy-done) | copy-start | bytes 3145732 | tf_op jit(solution)/shard_map/while
  440.1 3.8 copy-start
  459.8 9.8 %copy-start.1 = (bf16[32,128,128]{2,1,0:T(8,128)(2,1)S(1)}, bf16[32,128,128]{2,1,0:T(8,128)(2,1)}, u32[]{:S(2)}) copy-start(bf16[32,128,128]{2,1,0:T(8,128)(2,1)} %copy-done) | copy-start | bytes 3145732 | tf_op jit(solution)/shard_map/while
  469.6 3.8 copy-start
  489.3 9.7 %copy-start.1 = (bf16[32,128,128]{2,1,0:T(8,128)(2,1)S(1)}, bf16[32,128,128]{2,1,0:T(8,128)(2,1)}, u32[]{:S(2)}) copy-start(bf16[32,128,128]{2,1,0:T(8,128)(2,1)} %copy-done) | copy-start | bytes 3145732 | tf_op jit(solution)/shard_map/while
  499.0 54.6 %all-to-all-start.1 = ((f32[16,2,128,128]{3,2,1,0:T(8,128)}), f32[16,2,128,128]{3,2,1,0:T(8,128)S(1)}, u32[]{:S(2)}, u32[]{:S(2)}) async-start(f32[16,2,128,128]{3,2,1,0:T(8,128)} %bitcast.108), calls=%async_computation.1 | async-start | bytes 4194304 | tf_op jit(solution)/shard_map/all_to_all | solution.py:103
  506.2 223.1 %reduce-scatter.2.cloned.1.call-start = ((), (), s32[]{:S(2)}) async-start(), calls=%async_computation.4 | async-start | bytes 1081344 | tf_op jit(solution)/shard_map/reduce_scatter | solution.py:123
  508.5 383.6 %all-reduce.2.cloned.1.call-start = ((), (), s32[]{:S(2)}) async-start(), calls=%async_computation.3 | async-start | bytes 2097152 | tf_op jit(solution)/shard_map/psum | solution.py:115
  556.3 1.0 copy-start.2
Sparse Core Ops, SparseCore 0:
  114.8 92.5 all-gather.2
  511.4 217.8 reduce-scatter.1
  733.3 158.7 all-reduce.1
